TPU v7x, 256 devices: a whole 4x4x8 slice. The times are simulated.
256 devices in a mesh: gossip: 16 (over z, x_hi), shard: 16 (over y, x_lo, core).
Axes of the slice: x: 4 (x_hi: 2, x_lo: 2; x = x_hi * 2 + x_lo), y: 4, z: 8, core: 2. Of those that a mesh axis runs over, the one named last changes fastest.
Arguments:
- activations: bfloat16 [16, 2048, 2560], P('gossip', 'shard'), may hold values from -6 to 6
- out_grads: bfloat16 [16, 2048, 6912], P('gossip', 'shard'), may hold values from -0.13183594 to 0.13183594
- params: bfloat16 [16, 2560, 6912], P('gossip', 'shard'), may hold values from -6 to 6
- first_moment: bfloat16 [16, 2560, 6912], P('gossip', 'shard'), may hold values from -3 to 3
- second_moment: bfloat16 [16, 2560, 6912], P('gossip', 'shard'), may hold values from 0.0009994507 to 0.099609375
- gossip_round: int32 [1], replicated, may hold values from 0 to 2
- step_count: int32 [1], replicated, may hold values from 1 to 8
Outputs:
- averaged: bfloat16 [16, 2560, 6912], P('gossip', 'shard')
- new_moment: bfloat16 [16, 2560, 6912], P('gossip', 'shard')
All inputs are finite; a program needn't handle non-finite values.
Results may differ from a plain program's by a relative error of at most 0.001.
The roundings to bfloat16 on the way count: a program that leaves them out, or rounds other values in their place, can miss the bound.
Values may be sent and summed in bfloat16 or wider, within the bound.
No kernel may reach another device: no remote copies, remote signals or barrier semaphores. Data moves between devices by JAX's collectives and lax.ppermute only.
A program may use at most 128 MiB of HBM per device.

v0:
```python
from functools import partial

import jax
import jax.numpy as jnp
from jax import lax
from jax.sharding import PartitionSpec as P

ROUNDS = 3


def shortened(x):

    def short(part):
        return part.astype(jnp.bfloat16) if part.dtype == jnp.float32 else part

    return jax.tree.map(short, x)


def shifted(block, axis, distance):
    devices = range(lax.axis_size(axis))
    route = [((i - distance) % len(devices), i) for i in devices]
    return lax.ppermute(block, axis, route)


def send_over(stepped, offset):
    return jax.tree.map(
        lambda part, own: part.astype(own.dtype),
        shifted(shortened(stepped), "gossip", offset),
        stepped,
    )


def adam_rows(gradient, weight, moment_a, moment_b, bias_one, bias_two):
    moment_one = 0.9 * moment_a.astype(jnp.float32) + 0.1 * gradient
    moment_two = 0.999 * moment_b.astype(jnp.float32) + 0.001 * gradient * gradient
    update = moment_one / bias_one / (jnp.sqrt(moment_two / bias_two) + 1e-08)
    stepped = (weight.astype(jnp.float32) * (1.0 - 0.02 * 0.1) - 0.02 * update).astype(jnp.bfloat16)
    return (stepped, moment_one.astype(jnp.bfloat16))


def per_device(
    activations, out_grads, params, first_moment, second_moment, gossip_round, step_count
):
    columns = lax.all_to_all(activations, "shard", split_axis=2, concat_axis=1, tiled=True)
    act_block = columns[0]
    gradient = lax.dot_general(
        act_block,
        lax.all_gather(out_grads, "shard", axis=1, tiled=True)[0],
        (((0,), (0,)), ((), ())),
        preferred_element_type=jnp.float32,
    )
    count_float = step_count[0].astype(jnp.float32)
    bias_one = 1.0 - jnp.power(jnp.float32(0.9), count_float)
    bias_two = 1.0 - jnp.power(jnp.float32(0.999), count_float)
    stepped, moment_new = adam_rows(
        gradient, params[0], first_moment[0], second_moment[0], bias_one, bias_two
    )
    branches = [partial(send_over, offset=2**bit_number) for bit_number in range(ROUNDS)]
    received = lax.switch(gossip_round[0], branches, stepped)
    averaged = (0.5 * (stepped.astype(jnp.float32) + received.astype(jnp.float32))).astype(
        jnp.bfloat16
    )
    return (averaged[None], moment_new[None])


def solution(mesh):
    return jax.shard_map(
        per_device,
        mesh=mesh,
        in_specs=(
            P("gossip", "shard", None),
            P("gossip", "shard", None),
            P("gossip", "shard", None),
            P("gossip", "shard", None),
            P("gossip", "shard", None),
            P(),
            P(),
        ),
        out_specs=(P("gossip", "shard", None), P("gossip", "shard", None)),
        check_vma=False,
    )
```

profile of v0, /device:TPU:36, one launch (start us, length us, event | category | flops | bytes accessed | tf_op | source)
XLA Modules:
  0.0 246.3 jit_solution(9745936980700875281)
XLA Ops:
  7.2 0.0 all-gather.2.cloned.1.call-start
  7.2 0.7 all-gather.2.cloned.1.call-update
  7.9 2.5 %copy.11 = bf16[1,128,2560]{1,0,2:T(2,128)(2,1)S(1)} copy(bf16[1,128,2560]{2,1,0:T(8,128)(2,1)} %param.10) | data formatting | bytes 1310720 | tf_op args[0]
  10.4 0.5 broadcast.6
  10.9 14.3 %reduce = bf16[2560,128]{1,0:T(8,128)(2,1)S(1)} reduce(bf16[2560,1,128]{2,1,0:T(2,128)(2,1)S(1)} %bitcast.44, bf16[]{:T(256)} %broadcast.6), dimensions={1}, to_apply=%bitcast.38.reduce_sub_computation | reduce | bytes 1310722
  25.2 1.0 reshape.26
  26.2 5.2 %all-to-all-start = ((bf16[16,2,10240]{2,1,0:T(2,128)(2,1)}), bf16[16,2,10240]{2,1,0:T(2,128)(2,1)S(1)}, u32[]{:S(2)}, u32[]{:S(2)}) async-start(bf16[16,2,10240]{2,1,0:T(2,128)(2,1)} %reshape.26), calls=%async_computation | async-start | bytes 1310720 | tf_op jit(solution)/shard_map/all_to_all | solution.py:44
  32.8 18.2 %all-to-all-done = bf16[16,2,10240]{2,1,0:T(2,128)(2,1)S(1)} async-done(((bf16[16,2,10240]{2,1,0:T(2,128)(2,1)}), bf16[16,2,10240]{2,1,0:T(2,128)(2,1)S(1)}, u32[]{:S(2)}, u32[]{:S(2)}) %all-to-all-start) | async-done | bytes 655392 | tf_op jit(solution)/shard_map/all_to_all | solution.py:44
  51.0 0.6 reshape.27
  51.7 0.1 copy.13
  51.7 0.3 copy.12
  52.0 115.9 %all-gather.2.cloned.1.call-done = bf16[1,2048,6912]{2,1,0:T(8,128)(2,1)} async-done(((bf16[1,128,6912]{2,1,0:T(8,128)(2,1)}), bf16[1,2048,6912]{2,1,0:T(8,128)(2,1)}) %all-gather.2.cloned.1.call-update) | async-done | bytes 28311568 | tf_op jit(solution)/shard_map/all_gather | solution.py:48
  168.0 16.0 %fusion.10 = (bf16[1,160,6912]{2,1,0:T(8,128)(2,1)}, bf16[160,6912]{1,0:T(8,128)(2,1)S(1)}) fusion(bf16[1,160,6912]{2,1,0:T(8,128)(2,1)} %param.13, f32[]{:T(128)} %bitcast.6, bf16[1,160,6912]{2,1,0:T(8,128)(2,1)} %param.14, f32[]{:T(128)} %bitcast.4, bf16[1,160,6912]{2,1,0:T(8,128)(2,1)} %param.12, ...), kind=kOutput, calls=%fused_computation.14 | convolution fusion | flops 4550860800 | bytes 40026120 | tf_op jit(solution)/shard_map/dot_general | solution.py:46
  184.0 51.9 %conditional.4 = (bf16[160,6912]{1,0:T(8,128)(2,1)}) conditional(s32[]{:T(128)} %bitcast.7, bf16[160,6912]{1,0:T(8,128)(2,1)S(1)} %get-tuple-element.16, bf16[160,6912]{1,0:T(8,128)(2,1)S(1)} %get-tuple-element.16, bf16[160,6912]{1,0:T(8,128)(2,1)S(1)} %get-tuple-element.16), branch_computations={%region_0.0_spmd, %region_1.0_spmd, %region_2.0_spmd} | conditional | bytes 8847408
  184.0 1.5 collective-permute-start
  185.5 50.3 %collective-permute-done = bf16[160,6912]{1,0:T(8,128)(2,1)} collective-permute-done((bf16[160,6912]{1,0:T(8,128)(2,1)S(1)}, bf16[160,6912]{1,0:T(8,128)(2,1)}, u32[]{:S(2)}, u32[]{:S(2)}) %collective-permute-start) | collective-permute-done | bytes 2211872 | tf_op jit(solution)/shard_map/cond/branch_0_fun/ppermute | solution.py:22
  235.8 3.6 %fusion.11 = bf16[1,160,6912]{2,1,0:T(8,128)(2,1)} fusion(bf16[160,6912]{1,0:T(8,128)(2,1)} %get-tuple-element.17, bf16[160,6912]{1,0:T(8,128)(2,1)S(1)} %get-tuple-element.16), kind=kLoop, calls=%fused_computation.15 | loop fusion | flops 5529600 | bytes 6635520 | tf_op jit(solution)/shard_map/broadcast_in_dim | solution.py:63
Async XLA Ops:
  7.2 160.8 %all-gather.2.cloned.1.call-start = ((), (), s32[]{:S(2)}) async-start(), calls=%async_computation.1 | async-start | bytes 30081024 | tf_op jit(solution)/shard_map/all_gather | solution.py:48
  26.2 24.8 %all-to-all-start = ((bf16[16,2,10240]{2,1,0:T(2,128)(2,1)}), bf16[16,2,10240]{2,1,0:T(2,128)(2,1)S(1)}, u32[]{:S(2)}, u32[]{:S(2)}) async-start(bf16[16,2,10240]{2,1,0:T(2,128)(2,1)} %reshape.26), calls=%async_computation | async-start | bytes 1310720 | tf_op jit(solution)/shard_map/all_to_all | solution.py:44
  184.0 51.9 %collective-permute-start = (bf16[160,6912]{1,0:T(8,128)(2,1)S(1)}, bf16[160,6912]{1,0:T(8,128)(2,1)}, u32[]{:S(2)}, u32[]{:S(2)}) collective-permute-start(bf16[160,6912]{1,0:T(8,128)(2,1)S(1)} %param), channel_id=1, source_target_pairs={{240,0},{0,16},{16,32},{32,48},{48,64},{64,80},{80,96},{96,112},{1... | collective-permute-start | bytes 6635528 | tf_op jit(solution)/shard_map/cond/branch_0_fun/ppermute | solution.py:22
Sparse Core Ops, SparseCore 0:
  9.8 158.0 all-gather.1
where the time goes:
time: 250 us; the launch traced here: 246 us
  waiting for transfers between devices  185 us (74%)
  other arithmetic  17.9 us (7%)
  matrix products  16 us (6%)
  between operations  15.5 us (6%)
  starting transfers between devices  6.79 us (3%)
  local copies, waits for them, and re-layouts  4.99 us (2%)
    all_gather x1, waiting for transfers between devices, per_device(): lax.all_gather(out_grads, 'shard', axis=1, tiled=True)[0]  116 us
    ppermute x1, waiting for transfers between devices, shifted(): return lax.ppermute(block, axis, route)  50.3 us
    all_to_all x1, waiting for transfers between devices, per_device(): lax.all_to_all(activations, 'shard', split_axis=2, concat_axis=1, tiled=T...  18.2 us
    dot_general x1, matrix products, per_device(): lax.dot_general(act_block, lax.all_gather(out_grads, 'shard', axis=1, til...  16 us
    unnamed x1, other arithmetic  14.3 us
    all_to_all x1, starting transfers between devices, per_device(): lax.all_to_all(activations, 'shard', split_axis=2, concat_axis=1, tiled=T...  5.21 us
  transfers between devices with their start and end apart: 3, of which 3 were waited for; matrix products, arithmetic and copies ran while one was open for 8% of the time, Pallas kernels for 0%

commit v1 on v0

v1 whole, which is shorter than its diff:
```python
import functools
import math

import jax
import jax.numpy as jnp
from jax import lax
from jax.experimental import pallas as pl
from jax.experimental.pallas import tpu as pltpu
from jax.sharding import PartitionSpec as P

ROUNDS = 3
LANES = 128
WIDTHS = (5, 5, 4)
BF16 = jnp.bfloat16
F32 = jnp.float32
VMEM_LIMIT = 48 * 1024 * 1024

UNIT = 2.0**-12
CODE = 32767.0 / math.log1p(2.0**11 / UNIT)


def encode(g):
    level = jnp.log(1.0 + jnp.abs(g) * (1.0 / UNIT)) * CODE
    level = jnp.minimum(jnp.floor(level + 0.5), 32767.0)
    return jnp.where(g < 0.0, -level, level).astype(jnp.int32).astype(jnp.int16)


def decode(q):
    level = q.astype(jnp.int32).astype(F32)
    size = (jnp.exp(jnp.abs(level) * (1.0 / CODE)) - 1.0) * UNIT
    return jnp.where(level < 0.0, -size, size)


def chunks(total):
    out, at = [], 0
    for i, tiles in enumerate(WIDTHS):
        width = tiles * LANES
        if i == len(WIDTHS) - 1:
            at = total - 4 * width
        out.append((at, width))
        at += 4 * width
    return out


def params_of(**kw):
    return pltpu.CompilerParams(vmem_limit_bytes=VMEM_LIMIT, **kw)


SMEM = pl.BlockSpec(memory_space=pltpu.SMEM)
VMEM = pl.BlockSpec(memory_space=pltpu.VMEM)
HBM = pl.BlockSpec(memory_space=pl.ANY)


def cols(start, width):
    return pl.ds(pl.multiple_of(start, LANES), width)


def first_kernel(plan, place, act, dy, a0, a1, a2, a3, csend):
    y, c = place[0], place[2]
    rows = a0.shape[0]
    for r, out in enumerate((a0, a1, a2, a3)):
        quarter = lax.rem(y + r, 4)
        out[...] = act[:, cols(quarter * rows, rows)].T
    at = 0
    for start, width in plan:
        for x in range(2):
            csend[:, at : at + width] = dy[:, cols(start + (x * 2 + 1 - c) * width, width)]
            at += width


def split_kernel(plan, place, dy, crecv, *outs):
    x, c = place[1], place[2]
    tokens = dy.shape[0]
    at = 0
    for j, (start, width) in enumerate(plan):
        for far in range(2):
            side = x if far == 0 else 1 - x
            out = outs[2 * j + far]
            out[:tokens, :] = dy[:, cols(start + (side * 2 + c) * width, width)]
            out[tokens:, :] = crecv[:, cols(at + side * width, width)]
        at += 2 * width


def matmul_kernel(place, b0, bc, bx, bxc, *rest):
    pieces, outs = rest[:8], rest[8:12]
    lhs, rhs, acc, sems = rest[12:]
    x, c = place[1], place[2]
    quarter, tokens = b0.shape[1], b0.shape[2]
    copies = []
    for i in range(4):
        for k, b in enumerate((b0, bc, bx, bxc)):
            copies.append((b.at[i], lhs.at[:, (i * 4 + k) * tokens : (i * 4 + k + 1) * tokens]))
        for k in range(2):
            p = pieces[2 * i + k]
            depth = 2 * tokens
            copies.append((p, rhs.at[(2 * i + k) * depth : (2 * i + k + 1) * depth]))
    copies = [pltpu.make_async_copy(s, d, sems.at[n]) for n, (s, d) in enumerate(copies)]
    for copy in copies:
        copy.start()
    for copy in copies:
        copy.wait()
    acc[...] = jnp.dot(lhs[...], rhs[...], preferred_element_type=F32)
    rows = quarter // 4
    for k, out in enumerate(outs):
        dx, dc = k // 2, k % 2
        xx = x if dx == 0 else 1 - x
        cc = c if dc == 0 else 1 - c
        block = pl.ds(pl.multiple_of((xx * 2 + cc) * rows, 16), rows)
        out[...] = encode(acc[block, :])


def adam_kernel(start, width, n_prev, place, bias, *rest):
    g = rest[:4]
    params, first, second = rest[4:7]
    rest = rest[7 + n_prev :]
    stepped, moment, pv, fv, sv, mv, sems = rest
    x, c = place[1], place[2]
    rows = stepped.shape[0]
    window = pl.ds(start, 4 * width)
    loads = [
        pltpu.make_async_copy(src.at[:, window], dst, sems.at[n])
        for n, (src, dst) in enumerate(((params, pv), (first, fv), (second, sv)))
    ]
    for copy in loads:
        copy.start()
    for copy in loads:
        copy.wait()
    inv_one, inv_two = bias[0], bias[1]
    step = 32
    for k in range(4):
        dx, dc = k // 2, k % 2
        xx = x if dx == 0 else 1 - x
        cc = c if dc == 0 else 1 - c
        where = cols((xx * 2 + cc) * width, width)

        def body(i, _, k=k, where=where):
            r = pl.ds(pl.multiple_of(i * step, step), step)
            grad = decode(g[k][r, :])
            one = 0.9 * fv[r, where].astype(F32) + 0.1 * grad
            two = 0.999 * sv[r, where].astype(F32) + 0.001 * grad * grad
            update = (one * inv_one) / (jnp.sqrt(two * inv_two) + 1e-08)
            new = pv[r, where].astype(F32) * (1.0 - 0.02 * 0.1) - 0.02 * update
            stepped[r, where] = new.astype(BF16)
            mv[r, where] = one.astype(BF16)
            return 0

        lax.fori_loop(0, rows // step, body, 0)
    out = pltpu.make_async_copy(mv, moment.at[:, window], sems.at[3])
    out.start()
    out.wait()


def average_kernel(start, n_prev, own, other, *rest):
    averaged, buf, sem = rest[n_prev:]
    buf[...] = (0.5 * (own[...].astype(F32) + other[...].astype(F32))).astype(BF16)
    out = pltpu.make_async_copy(buf, averaged.at[:, pl.ds(start, buf.shape[1])], sem)
    out.start()
    out.wait()


def moved(block, dy=0, dx=0, dc=0):
    route = []
    for i in range(16):
        y, x, c = i // 4, i // 2 % 2, i % 2
        route.append((i, ((y + dy) % 4 * 2 + (x + dx) % 2) * 2 + (c + dc) % 2))
    return lax.ppermute(block, "shard", route)


def gossip(block, offset):
    return lax.ppermute(block, "gossip", [(i, (i + offset) % 16) for i in range(16)])


def body(offset, act, dy, params, first, second, place, bias):
    tokens, depth = act.shape
    total = dy.shape[1]
    rows = params.shape[0]
    quarter = depth // 4
    plan = chunks(total)
    half = sum(2 * w for _, w in plan)
    shape = jax.ShapeDtypeStruct
    with jax.named_scope("arrange"):
        a0, a1, a2, a3, csend = pl.pallas_call(
            functools.partial(first_kernel, plan),
            out_shape=[shape((quarter, tokens), BF16)] * 4 + [shape((tokens, half), BF16)],
            in_specs=[SMEM, VMEM, VMEM],
            out_specs=[VMEM] * 5,
            compiler_params=params_of(),
        )(place, act, dy)
        crecv = moved(csend, dc=1)
        split = pl.pallas_call(
            functools.partial(split_kernel, plan),
            out_shape=[shape((2 * tokens, w), BF16) for _, w in plan for _ in range(2)],
            in_specs=[SMEM, VMEM, VMEM],
            out_specs=[VMEM] * (2 * len(plan)),
            compiler_params=params_of(),
        )(place, dy, crecv)
    with jax.named_scope("activations"):
        b0 = jnp.stack([a0, moved(a1, dy=1), moved(a3, dy=3), moved(a2, dy=2)])
        bc = moved(b0, dc=1)
        bx = moved(b0, dx=1)
        bxc = moved(bx, dc=1)

    moment = averaged = None
    for j, (start, width) in enumerate(plan):
        with jax.named_scope("gather"):
            own = split[2 * j]
            far = moved(split[2 * j + 1], dx=1)
            own_l, own_r = moved(own, dy=1), moved(own, dy=3)
            far_l, far_r = moved(far, dy=1), moved(far, dy=3)
            own_o, far_o = moved(own_l, dy=1), moved(far_r, dy=3)
        pieces = (own, far, own_l, far_l, own_r, far_r, own_o, far_o)
        with jax.named_scope("gradient"):
            codes = pl.pallas_call(
                matmul_kernel,
                out_shape=[shape((rows, width), jnp.int16)] * 4,
                in_specs=[SMEM] + [HBM] * 12,
                out_specs=[VMEM] * 4,
                scratch_shapes=[
                    pltpu.VMEM((quarter, 16 * tokens), BF16),
                    pltpu.VMEM((16 * tokens, width), BF16),
                    pltpu.VMEM((quarter, width), F32),
                    pltpu.SemaphoreType.DMA((24,)),
                ],
                compiler_params=params_of(),
                cost_estimate=pl.CostEstimate(
                    flops=2 * quarter * width * 16 * tokens,
                    bytes_accessed=2 * 16 * tokens * (quarter + width),
                    transcendentals=quarter * width,
                ),
            )(place, b0, bc, bx, bxc, *pieces)
            grads = [
                codes[0],
                moved(codes[1], dc=1),
                moved(codes[2], dx=1),
                moved(codes[3], dx=1, dc=1),
            ]
        with jax.named_scope("adam"):
            previous = [] if moment is None else [moment]
            stepped, moment = pl.pallas_call(
                functools.partial(adam_kernel, start, width, len(previous)),
                out_shape=[shape((rows, 4 * width), BF16), shape((rows, total), BF16)],
                in_specs=[SMEM, SMEM] + [VMEM] * 4 + [HBM] * (3 + len(previous)),
                out_specs=[VMEM, HBM],
                scratch_shapes=[pltpu.VMEM((rows, 4 * width), BF16)] * 4
                + [pltpu.SemaphoreType.DMA((4,))],
                input_output_aliases={9: 1} if previous else {},
                compiler_params=params_of(),
                cost_estimate=pl.CostEstimate(
                    flops=100 * rows * width,
                    bytes_accessed=48 * rows * width,
                    transcendentals=12 * rows * width,
                ),
            )(place, bias, *grads, params, first, second, *previous)
        with jax.named_scope("average"):
            received = gossip(stepped, offset)
            previous = [] if averaged is None else [averaged]
            averaged = pl.pallas_call(
                functools.partial(average_kernel, start, len(previous)),
                out_shape=shape((rows, total), BF16),
                in_specs=[VMEM, VMEM] + [HBM] * len(previous),
                out_specs=HBM,
                scratch_shapes=[pltpu.VMEM((rows, 4 * width), BF16), pltpu.SemaphoreType.DMA],
                input_output_aliases={2: 0} if previous else {},
                compiler_params=params_of(),
                cost_estimate=pl.CostEstimate(
                    flops=12 * rows * width, bytes_accessed=24 * rows * width, transcendentals=0
                ),
            )(stepped, received, *previous)
    return averaged, moment


def per_device(
    activations, out_grads, params, first_moment, second_moment, gossip_round, step_count
):
    index = lax.axis_index("shard")
    place = jnp.stack([index // 4, index // 2 % 2, index % 2]).astype(jnp.int32)
    count_float = step_count[0].astype(F32)
    bias_one = 1.0 - jnp.power(F32(0.9), count_float)
    bias_two = 1.0 - jnp.power(F32(0.999), count_float)
    bias = jnp.stack([1.0 / bias_one, 1.0 / bias_two])
    averaged, moment = lax.switch(
        gossip_round[0],
        [functools.partial(body, 2**k) for k in range(ROUNDS)],
        activations[0],
        out_grads[0],
        params[0],
        first_moment[0],
        second_moment[0],
        place,
        bias,
    )
    return averaged[None], moment[None]


def solution(mesh):
    spec = P("gossip", "shard", None)
    return jax.shard_map(
        per_device,
        mesh=mesh,
        in_specs=(spec,) * 5 + (P(), P()),
        out_specs=(spec, spec),
        check_vma=False,
    )
```

time: 250 us -> 219 us (0.88); the launches traced: 246 us -> 218 us
  waiting for transfers between devices: 185 us -> 116 us
  starting transfers between devices: 6.79 us -> 55.4 us
  Pallas kernels: 0 us -> 33.2 us
  other arithmetic: 17.9 us -> 0.23 us
  matrix products: 16 us -> 0 us
  between operations: 15.5 us -> 3.19 us
  loops' own time: 0.01 us -> 9.91 us
  local copies, waits for them, and re-layouts: 4.99 us -> 0.01 us
    all_gather x1 -> x0, waiting for transfers between devices: 116 us -> none  [per_device(): lax.all_gather(out_grads, 'shard', axis=1, tiled=True)[0]]
    ppermute x1 -> x40, waiting for transfers between devices: 50.3 us -> 116 us  [the longest x37 100 us: moved(): return lax.ppermute(block, 'shard', route)]
    ppermute x1 -> x40, starting transfers between devices: 1.54 us -> 55.4 us  [the longest x37 50.4 us: moved(): return lax.ppermute(block, 'shard', route)]
    pallas_call x0 -> x11, Pallas kernels: none -> 33.2 us  [the longest x3 15.7 us: body(): pl.pallas_call(matmul_kernel, out_shape=[shape((rows, width), jnp.int16)]...]
    all_to_all x1 -> x0, waiting for transfers between devices: 18.2 us -> none  [per_device(): lax.all_to_all(activations, 'shard', split_axis=2, concat_axis=1, tiled=T...]
    dot_general x1 -> x0, matrix products: 16 us -> none  [per_device(): lax.dot_general(act_block, lax.all_gather(out_grads, 'shard', axis=1, til...]
    unnamed x1 -> x0, other arithmetic: 14.3 us -> none
    another operation x0 -> x1, loops' own time: none -> 9.91 us  [per_device(): lax.switch(gossip_round[0], [functools.partial(body, 2 ** k) for k in ran...]
  transfers between devices with their start and end apart: 3 -> 40, of which waited for: 3 -> 15; matrix products, arithmetic and copies ran while one was open for 8% -> 0% of each run, Pallas kernels for 0% -> 14%
where the time goes in v1:
time: 219 us; the launch traced here: 218 us
  waiting for transfers between devices  116 us (53%)
  starting transfers between devices  55.4 us (25%)
  Pallas kernels  33.2 us (15%)
  loops' own time  9.91 us (5%)
  between operations  3.19 us (1%)
    ppermute x37, waiting for transfers between devices, moved(): return lax.ppermute(block, 'shard', route)  100 us
    ppermute x37, starting transfers between devices, moved(): return lax.ppermute(block, 'shard', route)  50.4 us
    ppermute x3, waiting for transfers between devices, gossip(): lax.ppermute(block, 'gossip', [(i, (i + offset) % 16) for i in range(16)])  15.9 us
    pallas_call x3, Pallas kernels, body(): pl.pallas_call(matmul_kernel, out_shape=[shape((rows, width), jnp.int16)]...  15.7 us
    pallas_call x3, Pallas kernels, body(): pl.pallas_call(functools.partial(adam_kernel, start, width, len(previous)...  11.5 us
    another operation x1, loops' own time, per_device(): lax.switch(gossip_round[0], [functools.partial(body, 2 ** k) for k in ran...  9.91 us
    ppermute x3, starting transfers between devices, gossip(): lax.ppermute(block, 'gossip', [(i, (i + offset) % 16) for i in range(16)])  5.04 us
  transfers between devices with their start and end apart: 40, of which 15 were waited for; matrix products, arithmetic and copies ran while one was open for 0% of the time, Pallas kernels for 14%

profile of v1, /device:TPU:36, one launch (start us, length us, event | category | flops | bytes accessed | tf_op | source)
XLA Modules:
  0.0 218.0 jit_solution(9078610956311810204)
XLA Ops:
  2.3 214.6 %conditional.1 = (bf16[160,6912]{1,0:T(8,128)(2,1)}, bf16[1,160,6912]{2,1,0:T(8,128)(2,1)}) conditional(s32[]{:T(128)} %bitcast.30, (bf16[1,128,2560]{2,1,0:T(8,128)(2,1)}, bf16[1,128,6912]{2,1,0:T(8,128)(2,1)}, s32[3]{0:T(128)S(1)}, bf16[1,160,6912]{2,1,0:T(8,128)(2,1)}, bf16[1,160,6912]{2,1,0:T(8,128)(2,1)}, ...), branch_computations={%region_0.1_spmd, %region_1.2_spmd, %region_2.3_spmd} | conditional | flops 4730716160 | bytes 126027456 | solution.py:281
  2.3 2.1 arrange.6
  7.8 2.0 collective-permute-start.2
  9.8 2.6 %collective-permute-done = bf16[640,128]{1,0:T(8,128)(2,1)S(1)} collective-permute-done((bf16[640,128]{1,0:T(8,128)(2,1)S(1)}, bf16[640,128]{1,0:T(8,128)(2,1)S(1)}, u32[]{:S(2)}, u32[]{:S(2)}) %collective-permute-start) | collective-permute-done | bytes 163872 | tf_op jit(solution)/shard_map/cond/branch_0_fun/activations/ppermute | solution.py:166
  13.2 3.9 %collective-permute-done.2 = bf16[640,128]{1,0:T(8,128)(2,1)S(1)} collective-permute-done((bf16[640,128]{1,0:T(8,128)(2,1)S(1)}, bf16[640,128]{1,0:T(8,128)(2,1)S(1)}, u32[]{:S(2)}, u32[]{:S(2)}) %collective-permute-start.2) | collective-permute-done | bytes 163872 | tf_op jit(solution)/shard_map/cond/branch_0_fun/activations/ppermute | solution.py:166
  22.1 12.8 %collective-permute-done.4.bx = bf16[4,640,128]{2,1,0:T(8,128)(2,1)S(1)} collective-permute-done((bf16[4,640,128]{2,1,0:T(8,128)(2,1)S(1)}, bf16[4,640,128]{2,1,0:T(8,128)(2,1)S(1)}, u32[]{:S(2)}, u32[]{:S(2)}) %collective-permute-start.4) | collective-permute-done | bytes 655392 | tf_op jit(solution)/shard_map/cond/branch_0_fun/activations/ppermute | solution.py:166
  36.9 3.6 %collective-permute-done.7.rest_1_ = bf16[256,512]{1,0:T(8,128)(2,1)S(1)} collective-permute-done((bf16[256,512]{1,0:T(8,128)(2,1)S(1)}, bf16[256,512]{1,0:T(8,128)(2,1)S(1)}, u32[]{:S(2)}, u32[]{:S(2)}) %collective-permute-start.7) | collective-permute-done | bytes 262176 | tf_op jit(solution)/shard_map/cond/branch_0_fun/gather/ppermute | solution.py:166
  42.5 3.0 %collective-permute-start.30 = (bf16[256,640]{1,0:T(8,128)(2,1)S(1)}, bf16[256,640]{1,0:T(8,128)(2,1)S(1)}, u32[]{:S(2)}, u32[]{:S(2)}) collective-permute-start(bf16[256,640]{1,0:T(8,128)(2,1)S(1)} %get-tuple-element.82.rest_0_), channel_id=1, source_target_pairs={{0,12},{1,13},{2,14},{3,15},{4,0},{5,1},{6,2},{7,3},{8,4},{9,5},{1... | collective-permute-start | bytes 983048 | tf_op jit(solution)/shard_map/cond/branch_0_fun/gather/ppermute | solution.py:166
  45.5 2.0 collective-permute-done.17.rest_1_
  47.5 5.7 %collective-permute-done.27.rest_1_ = bf16[256,640]{1,0:T(8,128)(2,1)S(1)} collective-permute-done((bf16[256,640]{1,0:T(8,128)(2,1)S(1)}, bf16[256,640]{1,0:T(8,128)(2,1)S(1)}, u32[]{:S(2)}, u32[]{:S(2)}) %collective-permute-start.27) | collective-permute-done | bytes 327712 | tf_op jit(solution)/shard_map/cond/branch_0_fun/gather/ppermute | solution.py:166
  54.0 2.4 %collective-permute-start.11 = (bf16[256,512]{1,0:T(8,128)(2,1)S(1)}, bf16[256,512]{1,0:T(8,128)(2,1)S(1)}, u32[]{:S(2)}, u32[]{:S(2)}) collective-permute-start(bf16[256,512]{1,0:T(8,128)(2,1)S(1)} %collective-permute-done.7.rest_1_), channel_id=1, source_target_pairs={{0,12},{1,13},{2,14},{3,15},{4,0},{5,1},{6,2},{7,3},{8,4},{9,5},{1... | collective-permute-start | bytes 786440 | tf_op jit(solution)/shard_map/cond/branch_0_fun/gather/ppermute | solution.py:166
  56.9 1.9 collective-permute-start.9
  58.8 6.2 %collective-permute-done.28.rest_2_ = bf16[256,640]{1,0:T(8,128)(2,1)S(1)} collective-permute-done((bf16[256,640]{1,0:T(8,128)(2,1)S(1)}, bf16[256,640]{1,0:T(8,128)(2,1)S(1)}, u32[]{:S(2)}, u32[]{:S(2)}) %collective-permute-start.28) | collective-permute-done | bytes 327712 | tf_op jit(solution)/shard_map/cond/branch_0_fun/gather/ppermute | solution.py:166
  65.1 2.0 collective-permute-start.29
  67.0 3.6 %collective-permute-done.9.rest_3_ = bf16[256,512]{1,0:T(8,128)(2,1)S(1)} collective-permute-done((bf16[256,512]{1,0:T(8,128)(2,1)S(1)}, bf16[256,512]{1,0:T(8,128)(2,1)S(1)}, u32[]{:S(2)}, u32[]{:S(2)}) %collective-permute-start.9) | collective-permute-done | bytes 262176 | tf_op jit(solution)/shard_map/cond/branch_0_fun/gather/ppermute | solution.py:166
  70.6 3.2 %collective-permute-start.33 = (bf16[256,640]{1,0:T(8,128)(2,1)S(1)}, bf16[256,640]{1,0:T(8,128)(2,1)S(1)}, u32[]{:S(2)}, u32[]{:S(2)}) collective-permute-start(bf16[256,640]{1,0:T(8,128)(2,1)S(1)} %collective-permute-done.31.rest_5_), channel_id=1, source_target_pairs={{0,12},{1,13},{2,14},{3,15},{4,0},{5,1},{6,2},{7,3},{8,4},{9,5},{1... | collective-permute-start | bytes 983048 | tf_op jit(solution)/shard_map/cond/branch_0_fun/gather/ppermute | solution.py:166
  73.9 3.3 %collective-permute-done.21.rest_5_ = bf16[256,640]{1,0:T(8,128)(2,1)S(1)} collective-permute-done((bf16[256,640]{1,0:T(8,128)(2,1)S(1)}, bf16[256,640]{1,0:T(8,128)(2,1)S(1)}, u32[]{:S(2)}, u32[]{:S(2)}) %collective-permute-start.21) | collective-permute-done | bytes 327712 | tf_op jit(solution)/shard_map/cond/branch_0_fun/gather/ppermute | solution.py:166
  77.7 3.2 %collective-permute-start.23 = (bf16[256,640]{1,0:T(8,128)(2,1)S(1)}, bf16[256,640]{1,0:T(8,128)(2,1)S(1)}, u32[]{:S(2)}, u32[]{:S(2)}) collective-permute-start(bf16[256,640]{1,0:T(8,128)(2,1)S(1)} %collective-permute-done.21.rest_5_), channel_id=1, source_target_pairs={{0,12},{1,13},{2,14},{3,15},{4,0},{5,1},{6,2},{7,3},{8,4},{9,5},{1... | collective-permute-start | bytes 983048 | tf_op jit(solution)/shard_map/cond/branch_0_fun/gather/ppermute | solution.py:166
  80.9 3.8 %collective-permute-done.32.rest_6_ = bf16[256,640]{1,0:T(8,128)(2,1)S(1)} collective-permute-done((bf16[256,640]{1,0:T(8,128)(2,1)S(1)}, bf16[256,640]{1,0:T(8,128)(2,1)S(1)}, u32[]{:S(2)}, u32[]{:S(2)}) %collective-permute-start.32) | collective-permute-done | bytes 327712 | tf_op jit(solution)/shard_map/cond/branch_0_fun/gather/ppermute | solution.py:166
  84.7 3.2 %collective-permute-start.13 = (bf16[256,512]{1,0:T(8,128)(2,1)S(1)}, bf16[256,512]{1,0:T(8,128)(2,1)S(1)}, u32[]{:S(2)}, u32[]{:S(2)}) collective-permute-start(bf16[256,512]{1,0:T(8,128)(2,1)S(1)} %collective-permute-done.11.rest_5_), channel_id=1, source_target_pairs={{0,12},{1,13},{2,14},{3,15},{4,0},{5,1},{6,2},{7,3},{8,4},{9,5},{1... | collective-permute-start | bytes 786440 | tf_op jit(solution)/shard_map/cond/branch_0_fun/gather/ppermute | solution.py:166
  87.9 5.8 %gradient.11 = (s16[160,640]{1,0:T(8,128)(2,1)S(1)}, s16[160,640]{1,0:T(8,128)(2,1)S(1)}, s16[160,640]{1,0:T(8,128)(2,1)S(1)}, s16[160,640]{1,0:T(8,128)(2,1)S(1)}) custom-call(s32[3]{0:T(128)S(1)} %get-tuple-element.58.place, bf16[4,640,128]{2,1,0:T(8,128)(2,1)S(1)} %pad_maximum_fusion.b0, bf16[4,640,128]{2,1,0:T(8,128)(2,1)S(1)} %collective-permute-done.3.bc, ...), custom_call_target="tpu_custom_call" | custom-call | flops 1677721600 | bytes 5242880 | tf_op jit(solution)/shard_map/cond/branch_0_fun/gradient/pallas_call | solution.py:213
  93.8 4.9 %collective-permute-done.22.rest_6_ = bf16[256,640]{1,0:T(8,128)(2,1)S(1)} collective-permute-done((bf16[256,640]{1,0:T(8,128)(2,1)S(1)}, bf16[256,640]{1,0:T(8,128)(2,1)S(1)}, u32[]{:S(2)}, u32[]{:S(2)}) %collective-permute-start.22) | collective-permute-done | bytes 327712 | tf_op jit(solution)/shard_map/cond/branch_0_fun/gather/ppermute | solution.py:166
  98.7 11.4 %collective-permute-start.35 = (s16[160,640]{1,0:T(8,128)(2,1)S(1)}, s16[160,640]{1,0:T(8,128)(2,1)S(1)}, u32[]{:S(2)}, u32[]{:S(2)}) collective-permute-start(s16[160,640]{1,0:T(8,128)(2,1)S(1)} %get-tuple-element.86), channel_id=1, source_target_pairs={{0,2},{1,3},{2,0},{3,1},{4,6},{5,7},{6,4},{7,5},{8,10},{9,11},{10,... | collective-permute-start | bytes 614408 | tf_op jit(solution)/shard_map/cond/branch_0_fun/gradient/ppermute | solution.py:166
  110.1 5.8 %gradient.10 = (s16[160,640]{1,0:T(8,128)(2,1)S(1)}, s16[160,640]{1,0:T(8,128)(2,1)S(1)}, s16[160,640]{1,0:T(8,128)(2,1)S(1)}, s16[160,640]{1,0:T(8,128)(2,1)S(1)}) custom-call(s32[3]{0:T(128)S(1)} %get-tuple-element.58.place, bf16[4,640,128]{2,1,0:T(8,128)(2,1)S(1)} %pad_maximum_fusion.b0, bf16[4,640,128]{2,1,0:T(8,128)(2,1)S(1)} %collective-permute-done.3.bc, ...), custom_call_target="tpu_custom_call" | custom-call | flops 1677721600 | bytes 5242880 | tf_op jit(solution)/shard_map/cond/branch_0_fun/gradient/pallas_call | solution.py:213
  118.4 4.1 %gradient.9 = (s16[160,512]{1,0:T(8,128)(2,1)S(1)}, s16[160,512]{1,0:T(8,128)(2,1)S(1)}, s16[160,512]{1,0:T(8,128)(2,1)S(1)}, s16[160,512]{1,0:T(8,128)(2,1)S(1)}) custom-call(s32[3]{0:T(128)S(1)} %get-tuple-element.58.place, bf16[4,640,128]{2,1,0:T(8,128)(2,1)S(1)} %pad_maximum_fusion.b0, bf16[4,640,128]{2,1,0:T(8,128)(2,1)S(1)} %collective-permute-done.3.bc, ...), custom_call_target="tpu_custom_call" | custom-call | flops 1342177280 | bytes 4718592 | tf_op jit(solution)/shard_map/cond/branch_0_fun/gradient/pallas_call | solution.py:213
  124.5 4.0 %adam.9 = (bf16[160,2560]{1,0:T(8,128)(2,1)S(1)}, bf16[160,6912]{1,0:T(8,128)(2,1)}) custom-call(s32[3]{0:T(128)S(1)} %get-tuple-element.58.place, f32[2]{0:T(128)S(1)} %get-tuple-element.59.bias, s16[160,640]{1,0:T(8,128)(2,1)S(1)} %get-tuple-element.84.rest_0_, s16[160,640]{1,0:T(8,128)(2,1)S(1)} %collective-permute-done.34.rest_1_, ...), custom_call_target="tpu_custom_call" | custom-call | flops 10240000 | bytes 4915200 | tf_op jit(solution)/shard_map/cond/branch_0_fun/adam/pallas_call | solution.py:239
  128.9 2.0 collective-permute-start.39
  130.9 4.0 %adam.10 = (bf16[160,2560]{1,0:T(8,128)(2,1)S(1)}, bf16[160,6912]{1,0:T(8,128)(2,1)}) custom-call(s32[3]{0:T(128)S(1)} %get-tuple-element.58.place, f32[2]{0:T(128)S(1)} %get-tuple-element.59.bias, s16[160,640]{1,0:T(8,128)(2,1)S(1)} %get-tuple-element.78.rest_0_, ...), custom_call_target="tpu_custom_call", output_to_operand_aliasing={{1}: (9, {})} | custom-call | flops 10240000 | bytes 4915200 | tf_op jit(solution)/shard_map/cond/branch_0_fun/adam/pallas_call | solution.py:239
  135.0 3.0 %collective-permute-start.38 = (bf16[160,2560]{1,0:T(8,128)(2,1)S(1)}, bf16[160,2560]{1,0:T(8,128)(2,1)S(1)}, u32[]{:S(2)}, u32[]{:S(2)}) collective-permute-start(bf16[160,2560]{1,0:T(8,128)(2,1)S(1)} %get-tuple-element.92.own), channel_id=1, source_target_pairs={{0,16},{16,32},{32,48},{48,64},{64,80},{80,96},{96,112},{112,128},... | collective-permute-start | bytes 2457608 | tf_op jit(solution)/shard_map/cond/branch_0_fun/average/ppermute | solution.py:170
  137.9 46.4 %collective-permute-done.16.rest_3_ = s16[160,512]{1,0:T(8,128)(2,1)S(1)} collective-permute-done((s16[160,512]{1,0:T(8,128)(2,1)S(1)}, s16[160,512]{1,0:T(8,128)(2,1)S(1)}, u32[]{:S(2)}, u32[]{:S(2)}) %collective-permute-start.16) | collective-permute-done | bytes 163872 | tf_op jit(solution)/shard_map/cond/branch_0_fun/gradient/ppermute | solution.py:166
  184.4 3.4 %adam.11 = (bf16[160,2048]{1,0:T(8,128)(2,1)S(1)}, bf16[160,6912]{1,0:T(8,128)(2,1)}) custom-call(s32[3]{0:T(128)S(1)} %get-tuple-element.58.place, f32[2]{0:T(128)S(1)} %get-tuple-element.59.bias, s16[160,512]{1,0:T(8,128)(2,1)S(1)} %get-tuple-element.69.rest_0_, ...), custom_call_target="tpu_custom_call", output_to_operand_aliasing={{1}: (9, {})} | custom-call | flops 8192000 | bytes 3932160 | tf_op jit(solution)/shard_map/cond/branch_0_fun/adam/pallas_call | solution.py:239
  190.2 15.9 %collective-permute-done.37.other = bf16[160,2048]{1,0:T(8,128)(2,1)S(1)} collective-permute-done((bf16[160,2048]{1,0:T(8,128)(2,1)S(1)}, bf16[160,2048]{1,0:T(8,128)(2,1)S(1)}, u32[]{:S(2)}, u32[]{:S(2)}) %collective-permute-start.37) | collective-permute-done | bytes 655392 | tf_op jit(solution)/shard_map/cond/branch_0_fun/average/ppermute | solution.py:170
  (71 shorter events, 23.6 us)
Async XLA Ops:
  4.4 14.1 %collective-permute-start.6 = (bf16[128,3584]{1,0:T(8,128)(2,1)S(1)}, bf16[128,3584]{1,0:T(8,128)(2,1)S(1)}, u32[]{:S(2)}, u32[]{:S(2)}) collective-permute-start(bf16[128,3584]{1,0:T(8,128)(2,1)S(1)} %get-tuple-element.66), channel_id=1, source_target_pairs={{0,1},{1,0},{2,3},{3,2},{4,5},{5,4},{6,7},{7,6},{8,9},{9,8},{10,11... | collective-permute-start | bytes 2752520 | tf_op jit(solution)/shard_map/cond/branch_0_fun/arrange/ppermute | solution.py:166
  17.1 17.7 %collective-permute-start.4 = (bf16[4,640,128]{2,1,0:T(8,128)(2,1)S(1)}, bf16[4,640,128]{2,1,0:T(8,128)(2,1)S(1)}, u32[]{:S(2)}, u32[]{:S(2)}) collective-permute-start(bf16[4,640,128]{2,1,0:T(8,128)(2,1)S(1)} %pad_maximum_fusion.b0), channel_id=1, source_target_pairs={{0,2},{1,3},{2,0},{3,1},{4,6},{5,7},{6,4},{7,5},{8,10},{9,11},{10,... | collective-permute-start | bytes 1966088 | tf_op jit(solution)/shard_map/cond/branch_0_fun/activations/ppermute | solution.py:166
  18.4 17.6 %collective-permute-start.3 = (bf16[4,640,128]{2,1,0:T(8,128)(2,1)S(1)}, bf16[4,640,128]{2,1,0:T(8,128)(2,1)S(1)}, u32[]{:S(2)}, u32[]{:S(2)}) collective-permute-start(bf16[4,640,128]{2,1,0:T(8,128)(2,1)S(1)} %pad_maximum_fusion.b0), channel_id=1, source_target_pairs={{0,1},{1,0},{2,3},{3,2},{4,5},{5,4},{6,7},{7,6},{8,9},{9,8},{10,11... | collective-permute-start | bytes 1966088 | tf_op jit(solution)/shard_map/cond/branch_0_fun/activations/ppermute | solution.py:166
  19.1 21.4 %collective-permute-start.7 = (bf16[256,512]{1,0:T(8,128)(2,1)S(1)}, bf16[256,512]{1,0:T(8,128)(2,1)S(1)}, u32[]{:S(2)}, u32[]{:S(2)}) collective-permute-start(bf16[256,512]{1,0:T(8,128)(2,1)S(1)} %get-tuple-element.68), channel_id=1, source_target_pairs={{0,2},{1,3},{2,0},{3,1},{4,6},{5,7},{6,4},{7,5},{8,10},{9,11},{10,... | collective-permute-start | bytes 786440 | tf_op jit(solution)/shard_map/cond/branch_0_fun/gather/ppermute | solution.py:166
  20.0 22.2 %collective-permute-start.10 = (bf16[256,512]{1,0:T(8,128)(2,1)S(1)}, bf16[256,512]{1,0:T(8,128)(2,1)S(1)}, u32[]{:S(2)}, u32[]{:S(2)}) collective-permute-start(bf16[256,512]{1,0:T(8,128)(2,1)S(1)} %get-tuple-element.67.rest_0_), channel_id=1, source_target_pairs={{0,12},{1,13},{2,14},{3,15},{4,0},{5,1},{6,2},{7,3},{8,4},{9,5},{1... | collective-permute-start | bytes 786440 | tf_op jit(solution)/shard_map/cond/branch_0_fun/gather/ppermute | solution.py:166
  21.8 20.7 %collective-permute-start.8 = (bf16[256,512]{1,0:T(8,128)(2,1)S(1)}, bf16[256,512]{1,0:T(8,128)(2,1)S(1)}, u32[]{:S(2)}, u32[]{:S(2)}) collective-permute-start(bf16[256,512]{1,0:T(8,128)(2,1)S(1)} %get-tuple-element.67.rest_0_), channel_id=1, source_target_pairs={{0,4},{1,5},{2,6},{3,7},{4,8},{5,9},{6,10},{7,11},{8,12},{9,13},{1... | collective-permute-start | bytes 786440 | tf_op jit(solution)/shard_map/cond/branch_0_fun/gather/ppermute | solution.py:166
  34.9 12.6 %collective-permute-start.17 = (bf16[256,640]{1,0:T(8,128)(2,1)S(1)}, bf16[256,640]{1,0:T(8,128)(2,1)S(1)}, u32[]{:S(2)}, u32[]{:S(2)}) collective-permute-start(bf16[256,640]{1,0:T(8,128)(2,1)S(1)} %get-tuple-element.77), channel_id=1, source_target_pairs={{0,2},{1,3},{2,0},{3,1},{4,6},{5,7},{6,4},{7,5},{8,10},{9,11},{10,... | collective-permute-start | bytes 983048 | tf_op jit(solution)/shard_map/cond/branch_0_fun/gather/ppermute | solution.py:166
  36.1 17.1 %collective-permute-start.27 = (bf16[256,640]{1,0:T(8,128)(2,1)S(1)}, bf16[256,640]{1,0:T(8,128)(2,1)S(1)}, u32[]{:S(2)}, u32[]{:S(2)}) collective-permute-start(bf16[256,640]{1,0:T(8,128)(2,1)S(1)} %get-tuple-element.83), channel_id=1, source_target_pairs={{0,2},{1,3},{2,0},{3,1},{4,6},{5,7},{6,4},{7,5},{8,10},{9,11},{10,... | collective-permute-start | bytes 983048 | tf_op jit(solution)/shard_map/cond/branch_0_fun/gather/ppermute | solution.py:166
  40.5 13.5 %collective-permute-start.20 = (bf16[256,640]{1,0:T(8,128)(2,1)S(1)}, bf16[256,640]{1,0:T(8,128)(2,1)S(1)}, u32[]{:S(2)}, u32[]{:S(2)}) collective-permute-start(bf16[256,640]{1,0:T(8,128)(2,1)S(1)} %get-tuple-element.76.rest_0_), channel_id=1, source_target_pairs={{0,12},{1,13},{2,14},{3,15},{4,0},{5,1},{6,2},{7,3},{8,4},{9,5},{1... | collective-permute-start | bytes 983048 | tf_op jit(solution)/shard_map/cond/branch_0_fun/gather/ppermute | solution.py:166
  42.3 14.1 %collective-permute-start.18 = (bf16[256,640]{1,0:T(8,128)(2,1)S(1)}, bf16[256,640]{1,0:T(8,128)(2,1)S(1)}, u32[]{:S(2)}, u32[]{:S(2)}) collective-permute-start(bf16[256,640]{1,0:T(8,128)(2,1)S(1)} %get-tuple-element.76.rest_0_), channel_id=1, source_target_pairs={{0,4},{1,5},{2,6},{3,7},{4,8},{5,9},{6,10},{7,11},{8,12},{9,13},{1... | collective-permute-start | bytes 983048 | tf_op jit(solution)/shard_map/cond/branch_0_fun/gather/ppermute | solution.py:166
  42.5 14.3 %collective-permute-start.30 = (bf16[256,640]{1,0:T(8,128)(2,1)S(1)}, bf16[256,640]{1,0:T(8,128)(2,1)S(1)}, u32[]{:S(2)}, u32[]{:S(2)}) collective-permute-start(bf16[256,640]{1,0:T(8,128)(2,1)S(1)} %get-tuple-element.82.rest_0_), channel_id=1, source_target_pairs={{0,12},{1,13},{2,14},{3,15},{4,0},{5,1},{6,2},{7,3},{8,4},{9,5},{1... | collective-permute-start | bytes 983048 | tf_op jit(solution)/shard_map/cond/branch_0_fun/gather/ppermute | solution.py:166
  47.5 26.4 %collective-permute-start.5 = (bf16[4,640,128]{2,1,0:T(8,128)(2,1)S(1)}, bf16[4,640,128]{2,1,0:T(8,128)(2,1)S(1)}, u32[]{:S(2)}, u32[]{:S(2)}) collective-permute-start(bf16[4,640,128]{2,1,0:T(8,128)(2,1)S(1)} %collective-permute-done.4.bx), channel_id=1, source_target_pairs={{0,1},{1,0},{2,3},{3,2},{4,5},{5,4},{6,7},{7,6},{8,9},{9,8},{10,11... | collective-permute-start | bytes 1966088 | tf_op jit(solution)/shard_map/cond/branch_0_fun/activations/ppermute | solution.py:166
  56.4 14.2 %collective-permute-start.31 = (bf16[256,640]{1,0:T(8,128)(2,1)S(1)}, bf16[256,640]{1,0:T(8,128)(2,1)S(1)}, u32[]{:S(2)}, u32[]{:S(2)}) collective-permute-start(bf16[256,640]{1,0:T(8,128)(2,1)S(1)} %collective-permute-done.27.rest_1_), channel_id=1, source_target_pairs={{0,12},{1,13},{2,14},{3,15},{4,0},{5,1},{6,2},{7,3},{8,4},{9,5},{1... | collective-permute-start | bytes 983048 | tf_op jit(solution)/shard_map/cond/branch_0_fun/gather/ppermute | solution.py:166
  56.9 13.8 %collective-permute-start.9 = (bf16[256,512]{1,0:T(8,128)(2,1)S(1)}, bf16[256,512]{1,0:T(8,128)(2,1)S(1)}, u32[]{:S(2)}, u32[]{:S(2)}) collective-permute-start(bf16[256,512]{1,0:T(8,128)(2,1)S(1)} %collective-permute-done.7.rest_1_), channel_id=1, source_target_pairs={{0,4},{1,5},{2,6},{3,7},{4,8},{5,9},{6,10},{7,11},{8,12},{9,13},{1... | collective-permute-start | bytes 786440 | tf_op jit(solution)/shard_map/cond/branch_0_fun/gather/ppermute | solution.py:166
  70.6 14.0 %collective-permute-start.32 = (bf16[256,640]{1,0:T(8,128)(2,1)S(1)}, bf16[256,640]{1,0:T(8,128)(2,1)S(1)}, u32[]{:S(2)}, u32[]{:S(2)}) collective-permute-start(bf16[256,640]{1,0:T(8,128)(2,1)S(1)} %collective-permute-done.28.rest_2_), channel_id=1, source_target_pairs={{0,4},{1,5},{2,6},{3,7},{4,8},{5,9},{6,10},{7,11},{8,12},{9,13},{1... | collective-permute-start | bytes 983048 | tf_op jit(solution)/shard_map/cond/branch_0_fun/gather/ppermute | solution.py:166
  70.6 14.1 %collective-permute-start.33 = (bf16[256,640]{1,0:T(8,128)(2,1)S(1)}, bf16[256,640]{1,0:T(8,128)(2,1)S(1)}, u32[]{:S(2)}, u32[]{:S(2)}) collective-permute-start(bf16[256,640]{1,0:T(8,128)(2,1)S(1)} %collective-permute-done.31.rest_5_), channel_id=1, source_target_pairs={{0,12},{1,13},{2,14},{3,15},{4,0},{5,1},{6,2},{7,3},{8,4},{9,5},{1... | collective-permute-start | bytes 983048 | tf_op jit(solution)/shard_map/cond/branch_0_fun/gather/ppermute | solution.py:166
  73.9 19.8 %collective-permute-start.19 = (bf16[256,640]{1,0:T(8,128)(2,1)S(1)}, bf16[256,640]{1,0:T(8,128)(2,1)S(1)}, u32[]{:S(2)}, u32[]{:S(2)}) collective-permute-start(bf16[256,640]{1,0:T(8,128)(2,1)S(1)} %collective-permute-done.17.rest_1_), channel_id=1, source_target_pairs={{0,4},{1,5},{2,6},{3,7},{4,8},{5,9},{6,10},{7,11},{8,12},{9,13},{1... | collective-permute-start | bytes 983048 | tf_op jit(solution)/shard_map/cond/branch_0_fun/gather/ppermute | solution.py:166
  77.2 21.5 %collective-permute-start.22 = (bf16[256,640]{1,0:T(8,128)(2,1)S(1)}, bf16[256,640]{1,0:T(8,128)(2,1)S(1)}, u32[]{:S(2)}, u32[]{:S(2)}) collective-permute-start(bf16[256,640]{1,0:T(8,128)(2,1)S(1)} %collective-permute-done.18.rest_2_), channel_id=1, source_target_pairs={{0,4},{1,5},{2,6},{3,7},{4,8},{5,9},{6,10},{7,11},{8,12},{9,13},{1... | collective-permute-start | bytes 983048 | tf_op jit(solution)/shard_map/cond/branch_0_fun/gather/ppermute | solution.py:166
  77.7 32.5 %collective-permute-start.23 = (bf16[256,640]{1,0:T(8,128)(2,1)S(1)}, bf16[256,640]{1,0:T(8,128)(2,1)S(1)}, u32[]{:S(2)}, u32[]{:S(2)}) collective-permute-start(bf16[256,640]{1,0:T(8,128)(2,1)S(1)} %collective-permute-done.21.rest_5_), channel_id=1, source_target_pairs={{0,12},{1,13},{2,14},{3,15},{4,0},{5,1},{6,2},{7,3},{8,4},{9,5},{1... | collective-permute-start | bytes 983048 | tf_op jit(solution)/shard_map/cond/branch_0_fun/gather/ppermute | solution.py:166
  84.7 31.2 %collective-permute-start.12 = (bf16[256,512]{1,0:T(8,128)(2,1)S(1)}, bf16[256,512]{1,0:T(8,128)(2,1)S(1)}, u32[]{:S(2)}, u32[]{:S(2)}) collective-permute-start(bf16[256,512]{1,0:T(8,128)(2,1)S(1)} %collective-permute-done.8.rest_2_), channel_id=1, source_target_pairs={{0,4},{1,5},{2,6},{3,7},{4,8},{5,9},{6,10},{7,11},{8,12},{9,13},{1... | collective-permute-start | bytes 786440 | tf_op jit(solution)/shard_map/cond/branch_0_fun/gather/ppermute | solution.py:166
  84.7 32.2 %collective-permute-start.13 = (bf16[256,512]{1,0:T(8,128)(2,1)S(1)}, bf16[256,512]{1,0:T(8,128)(2,1)S(1)}, u32[]{:S(2)}, u32[]{:S(2)}) collective-permute-start(bf16[256,512]{1,0:T(8,128)(2,1)S(1)} %collective-permute-done.11.rest_5_), channel_id=1, source_target_pairs={{0,12},{1,13},{2,14},{3,15},{4,0},{5,1},{6,2},{7,3},{8,4},{9,5},{1... | collective-permute-start | bytes 786440 | tf_op jit(solution)/shard_map/cond/branch_0_fun/gather/ppermute | solution.py:166
  93.7 24.4 %collective-permute-start.34 = (s16[160,640]{1,0:T(8,128)(2,1)S(1)}, s16[160,640]{1,0:T(8,128)(2,1)S(1)}, u32[]{:S(2)}, u32[]{:S(2)}) collective-permute-start(s16[160,640]{1,0:T(8,128)(2,1)S(1)} %get-tuple-element.85), channel_id=1, source_target_pairs={{0,1},{1,0},{2,3},{3,2},{4,5},{5,4},{6,7},{7,6},{8,9},{9,8},{10,11... | collective-permute-start | bytes 614408 | tf_op jit(solution)/shard_map/cond/branch_0_fun/gradient/ppermute | solution.py:166
  98.7 23.8 %collective-permute-start.35 = (s16[160,640]{1,0:T(8,128)(2,1)S(1)}, s16[160,640]{1,0:T(8,128)(2,1)S(1)}, u32[]{:S(2)}, u32[]{:S(2)}) collective-permute-start(s16[160,640]{1,0:T(8,128)(2,1)S(1)} %get-tuple-element.86), channel_id=1, source_target_pairs={{0,2},{1,3},{2,0},{3,1},{4,6},{5,7},{6,4},{7,5},{8,10},{9,11},{10,... | collective-permute-start | bytes 614408 | tf_op jit(solution)/shard_map/cond/branch_0_fun/gradient/ppermute | solution.py:166
  110.1 13.2 %collective-permute-start.36 = (s16[160,640]{1,0:T(8,128)(2,1)S(1)}, s16[160,640]{1,0:T(8,128)(2,1)S(1)}, u32[]{:S(2)}, u32[]{:S(2)}) collective-permute-start(s16[160,640]{1,0:T(8,128)(2,1)S(1)} %get-tuple-element.87), channel_id=1, source_target_pairs={{0,3},{1,2},{2,1},{3,0},{4,7},{5,6},{6,5},{7,4},{8,11},{9,10},{10,... | collective-permute-start | bytes 614408 | tf_op jit(solution)/shard_map/cond/branch_0_fun/gradient/ppermute | solution.py:166
  115.9 12.7 %collective-permute-start.24 = (s16[160,640]{1,0:T(8,128)(2,1)S(1)}, s16[160,640]{1,0:T(8,128)(2,1)S(1)}, u32[]{:S(2)}, u32[]{:S(2)}) collective-permute-start(s16[160,640]{1,0:T(8,128)(2,1)S(1)} %get-tuple-element.79), channel_id=1, source_target_pairs={{0,1},{1,0},{2,3},{3,2},{4,5},{5,4},{6,7},{7,6},{8,9},{9,8},{10,11... | collective-permute-start | bytes 614408 | tf_op jit(solution)/shard_map/cond/branch_0_fun/gradient/ppermute | solution.py:166
  118.1 12.8 %collective-permute-start.26 = (s16[160,640]{1,0:T(8,128)(2,1)S(1)}, s16[160,640]{1,0:T(8,128)(2,1)S(1)}, u32[]{:S(2)}, u32[]{:S(2)}) collective-permute-start(s16[160,640]{1,0:T(8,128)(2,1)S(1)} %get-tuple-element.81), channel_id=1, source_target_pairs={{0,3},{1,2},{2,1},{3,0},{4,7},{5,6},{6,5},{7,4},{8,11},{9,10},{10,... | collective-permute-start | bytes 614408 | tf_op jit(solution)/shard_map/cond/branch_0_fun/gradient/ppermute | solution.py:166
  122.5 15.4 %collective-permute-start.14 = (s16[160,512]{1,0:T(8,128)(2,1)S(1)}, s16[160,512]{1,0:T(8,128)(2,1)S(1)}, u32[]{:S(2)}, u32[]{:S(2)}) collective-permute-start(s16[160,512]{1,0:T(8,128)(2,1)S(1)} %get-tuple-element.70), channel_id=1, source_target_pairs={{0,1},{1,0},{2,3},{3,2},{4,5},{5,4},{6,7},{7,6},{8,9},{9,8},{10,11... | collective-permute-start | bytes 491528 | tf_op jit(solution)/shard_map/cond/branch_0_fun/gradient/ppermute | solution.py:166
  123.3 14.6 %collective-permute-start.15 = (s16[160,512]{1,0:T(8,128)(2,1)S(1)}, s16[160,512]{1,0:T(8,128)(2,1)S(1)}, u32[]{:S(2)}, u32[]{:S(2)}) collective-permute-start(s16[160,512]{1,0:T(8,128)(2,1)S(1)} %get-tuple-element.71), channel_id=1, source_target_pairs={{0,2},{1,3},{2,0},{3,1},{4,6},{5,7},{6,4},{7,5},{8,10},{9,11},{10,... | collective-permute-start | bytes 491528 | tf_op jit(solution)/shard_map/cond/branch_0_fun/gradient/ppermute | solution.py:166
  128.6 55.8 %collective-permute-start.16 = (s16[160,512]{1,0:T(8,128)(2,1)S(1)}, s16[160,512]{1,0:T(8,128)(2,1)S(1)}, u32[]{:S(2)}, u32[]{:S(2)}) collective-permute-start(s16[160,512]{1,0:T(8,128)(2,1)S(1)} %get-tuple-element.72), channel_id=1, source_target_pairs={{0,3},{1,2},{2,1},{3,0},{4,7},{5,6},{6,5},{7,4},{8,11},{9,10},{10,... | collective-permute-start | bytes 491528 | tf_op jit(solution)/shard_map/cond/branch_0_fun/gradient/ppermute | solution.py:166
  128.9 59.0 %collective-permute-start.39 = (bf16[160,2560]{1,0:T(8,128)(2,1)S(1)}, bf16[160,2560]{1,0:T(8,128)(2,1)S(1)}, u32[]{:S(2)}, u32[]{:S(2)}) collective-permute-start(bf16[160,2560]{1,0:T(8,128)(2,1)S(1)} %get-tuple-element.93.own), channel_id=1, source_target_pairs={{0,16},{16,32},{32,48},{48,64},{64,80},{80,96},{96,112},{112,128},... | collective-permute-start | bytes 2457608 | tf_op jit(solution)/shard_map/cond/branch_0_fun/average/ppermute | solution.py:170
  135.0 54.1 %collective-permute-start.38 = (bf16[160,2560]{1,0:T(8,128)(2,1)S(1)}, bf16[160,2560]{1,0:T(8,128)(2,1)S(1)}, u32[]{:S(2)}, u32[]{:S(2)}) collective-permute-start(bf16[160,2560]{1,0:T(8,128)(2,1)S(1)} %get-tuple-element.92.own), channel_id=1, source_target_pairs={{0,16},{16,32},{32,48},{48,64},{64,80},{80,96},{96,112},{112,128},... | collective-permute-start | bytes 2457608 | tf_op jit(solution)/shard_map/cond/branch_0_fun/average/ppermute | solution.py:170
  187.8 18.3 %collective-permute-start.37 = (bf16[160,2048]{1,0:T(8,128)(2,1)S(1)}, bf16[160,2048]{1,0:T(8,128)(2,1)S(1)}, u32[]{:S(2)}, u32[]{:S(2)}) collective-permute-start(bf16[160,2048]{1,0:T(8,128)(2,1)S(1)} %get-tuple-element.91.own), channel_id=1, source_target_pairs={{0,16},{16,32},{32,48},{48,64},{64,80},{80,96},{96,112},{112,128},... | collective-permute-start | bytes 1966088 | tf_op jit(solution)/shard_map/cond/branch_0_fun/average/ppermute | solution.py:170
  (12 other events, 127.2 us)
